TPU v7x, 32 devices: a whole 2x2x4 slice. The times are simulated.
32 devices in a mesh: groups: 2 (over y), pb: 8 (over z, core), fc: 2 (over x), br: 1.
Axes of the slice: x: 2, y: 2, z: 4, core: 2. Of those that a mesh axis runs over, the one named last changes fastest.
Arguments:
- eigen_vectors: bfloat16 [64, 288, 288], P(('groups', 'pb'), 'br'), parts along dimension 0, may hold values from -0.375 to 0.375
- frequencies: bfloat16 [64, 288], P(('groups', 'pb'), 'br'), parts along dimension 0, may hold values from 0.35 to 0.49
- force_consts: bfloat16 [96, 3, 576], replicated, may hold values from -40 to 40
- neighbors: int32 [96, 8], replicated, may hold values from 0 to 95
- rotations: int32 [48, 3, 3], replicated, may hold values from -1 to 1, as said below
- atom_maps: int32 [48, 96], replicated, may hold values from 0 to 95, each once within a row
- grid_counts: int32 [16], P('groups'), parts along dimension 0, may hold values from 1 to 3, 12 in all
- trip_partners: int32 [24, 2], P('groups'), parts along dimension 0, may hold values from 1 to 31, as said below
- trip_turns: int32 [24, 2], P('groups'), parts along dimension 0, may hold values from 0 to 47
- trip_weights: int32 [24], P('groups'), parts along dimension 0, may hold values from 1 to 8
Outputs:
- linewidths: float32 [16, 288], P(('groups', 'pb')), parts along dimension 0
There are 2 independent parts, one for each index of `groups`. A program takes and returns all parts, laid end to end along the dimension named above; an argument that names none is the same for every part. Nothing has to cross between parts.
Inputs may be any that keep to these rules, and one draw needn't show every extreme that they name: Each grid point has at least one triplet; the triplets of grid point g are rows start[g] to start[g] + grid_counts[g] - 1 of the triplet tables; the counts sum to 12. `trip_partners`: every table index that is not a multiple of 4 is named exactly once; multiples of 4 are grid points and are never partners. `rotations`: each matrix is a signed permutation of the three axes. `atom_maps`: each row is a permutation of the atoms.
All inputs are finite; a program needn't handle non-finite values.
Results may differ from a plain program's by a relative error of at most 0.0003.
Values may be sent and summed in bfloat16 or wider, within the bound.
A program may use at most 128 MiB of HBM per device.

v0:
```python
import math

import jax
import jax.numpy as jnp
from jax import lax
from jax.experimental import pallas as pl
from jax.experimental.pallas import tpu as pltpu
from jax.sharding import PartitionSpec as P

SMEAR_WIDTH = 0.1
LEVELS = 128
GROUP = 8


def occupation(omega):
    return 1.0 / jnp.expm1(omega)


def columns_operator(turned, mapping, neighbors):
    atoms, slots = neighbors.shape
    target = mapping[neighbors]
    comp = jnp.arange(3 * atoms, dtype=jnp.int32)
    hit = target[:, :, None, None] == (comp // 3)[None, None, None, :]
    axes = jnp.tile(turned, (1, atoms))
    rows = jnp.where(hit, axes[None, None, :, :], 0)
    return rows.astype(jnp.bfloat16).reshape(3 * atoms * slots, 3 * atoms)


def unit_kernel(
    left_ref, right_ref, forces_ref, home_ref, at_ref, bt_ref, u1_ref, v1_ref, u2_ref, v2_ref,
    out_ref, half_main, half_tail, red_0, red_1, red_tail, squares, weights,
):
    atoms, rows, width = left_ref.shape[1:]
    comps = 3 * atoms
    modes = right_ref.shape[3]
    tail = modes - 256

    def halves(step, _):
        for inner in range(8):
            a = step * 8 + inner
            h = jnp.dot(forces_ref[a], right_ref[0, a], preferred_element_type=jnp.float32)
            parts = [h[x * width : (x + 1) * width] for x in range(3)]
            half_main[a] = jnp.concatenate([p[:, :256] for p in parts], axis=1).astype(jnp.bfloat16)
            ends = [p[:, 256:] for p in parts]
            ends.append(jnp.zeros((width, 128 - 3 * tail), jnp.float32))
            half_tail[a] = jnp.concatenate(ends, axis=1).astype(jnp.bfloat16)
        return 0

    lax.fori_loop(0, atoms // 8, halves, 0)

    def reduce_atoms(step, _):
        for inner in range(8):
            a = step * 8 + inner
            left = left_ref[0, a]
            main = jnp.dot(left, half_main[a], preferred_element_type=jnp.float32)
            ends = jnp.dot(left, half_tail[a], preferred_element_type=jnp.float32)
            for x in range(3):
                where = pl.ds(x * atoms + a, rows, stride=comps)
                red_0[where, :] = main[:, x * 256 : x * 256 + 128]
                red_1[where, :] = main[:, x * 256 + 128 : x * 256 + 256]
            red_tail[pl.ds(a, rows, stride=atoms), :] = ends
        return 0

    lax.fori_loop(0, atoms // 8, reduce_atoms, 0)

    def weigh(spot, a_col, b_col, u1, v1, u2, v2):
        q = u1 * (a_col * u2 - b_col * v2) + v1 * (b_col * u2 - a_col * v2)
        high = q.astype(jnp.bfloat16)
        low = (q - high.astype(jnp.float32)).astype(jnp.bfloat16)
        weights[spot, :LEVELS] = high
        weights[spot, LEVELS:] = low

    out_ref[0] = jnp.zeros(out_ref.shape[1:], jnp.float32)

    def group(g, _):
        home = home_ref[0]
        pieces = [[], [], []]
        for inner in range(GROUP):
            j = g * GROUP + inner
            a_col = at_ref[0, g][:, inner : inner + 1]
            b_col = bt_ref[0, g][:, inner : inner + 1]
            u1 = u1_ref[0, pl.ds(j, 1), :]
            v1 = v1_ref[0, pl.ds(j, 1), :]
            weigh(slice(inner * 256, inner * 256 + 256), a_col[:256], b_col[:256], u1, v1,
                  u2_ref[0, :256], v2_ref[0, :256])
            weigh(slice(GROUP * 256 + inner * tail, GROUP * 256 + (inner + 1) * tail),
                  a_col[256:], b_col[256:], u1, v1, u2_ref[0, 256:], v2_ref[0, 256:])
            base = pl.multiple_of(j * comps, comps)
            block = jnp.concatenate(
                [red_0[pl.ds(base, comps), :], red_1[pl.ds(base, comps), :]], axis=1
            ).astype(jnp.bfloat16)
            coupling = jnp.dot(home, block, preferred_element_type=jnp.float32)
            squares[:, inner * 256 : inner * 256 + 256] = (coupling * coupling).astype(jnp.bfloat16)
            ends = red_tail[pl.ds(pl.multiple_of(j * atoms, atoms), atoms), :]
            for x in range(3):
                pieces[x].append(ends[:, x * tail : (x + 1) * tail])
        block = jnp.concatenate(
            [jnp.concatenate(p, axis=1) for p in pieces], axis=0
        ).astype(jnp.bfloat16)
        coupling = jnp.dot(home, block, preferred_element_type=jnp.float32)
        squares[:, GROUP * 256 :] = (coupling * coupling).astype(jnp.bfloat16)
        out_ref[0] += jnp.dot(squares[...], weights[...], preferred_element_type=jnp.float32)
        return 0

    lax.fori_loop(0, rows // GROUP, group, 0)


def shards(
    eigen_vectors,
    frequencies,
    force_consts,
    neighbors,
    rotations,
    atom_maps,
    grid_counts,
    trip_partners,
    trip_turns,
    trip_weights,
):
    pb_count, fc_count, br_count = (lax.axis_size(n) for n in ("pb", "fc", "br"))
    devices = pb_count * fc_count * br_count
    me = (lax.axis_index("pb") * fc_count + lax.axis_index("fc")) * br_count + lax.axis_index("br")
    held = eigen_vectors.shape[0]
    modes = eigen_vectors.shape[1] * br_count
    comps = eigen_vectors.shape[2]
    atoms, slots = neighbors.shape
    width = 3 * slots
    trips = trip_weights.shape[0]
    common = math.gcd(trips, devices)
    cuts = devices // common
    units = trips // common
    block = modes // cuts
    rows = -(-block // GROUP) * GROUP
    groups = rows // GROUP
    f32 = jnp.float32

    table = lax.all_gather(eigen_vectors, "pb", axis=0, tiled=True)
    freq_table = lax.all_gather(frequencies, "pb", axis=0, tiled=True)
    if br_count > 1:
        table = lax.all_gather(table, "br", axis=1, tiled=True)
        freq_table = lax.all_gather(freq_table, "br", axis=1, tiled=True)

    starts = jnp.cumsum(grid_counts) - grid_counts
    ids = me * units + jnp.arange(units, dtype=jnp.int32)
    trip = ids // cuts
    first = ids % cuts * block
    owner = jnp.sum((starts[None, :] <= trip[:, None]).astype(jnp.int32), axis=1) - 1

    def rows_of(u):
        t = trip[u]
        left_q, right_q = trip_partners[t, 0], trip_partners[t, 1]
        left = lax.dynamic_slice(table, (left_q, first[u], 0), (1, block, comps))[0]
        left_f = lax.dynamic_slice(freq_table, (left_q, first[u]), (1, block))[0]
        home = lax.dynamic_index_in_dim(table, owner[u] * held, 0, False)
        home_f = lax.dynamic_index_in_dim(freq_table, owner[u] * held, 0, False)
        right = lax.dynamic_index_in_dim(table, right_q, 0, False)
        right_f = lax.dynamic_index_in_dim(freq_table, right_q, 0, False)
        return left, left_f, home, home_f, right, right_f

    picked = [jnp.stack(p) for p in zip(*[rows_of(u) for u in range(units)])]
    left, left_f, home, home_f, right, right_f = picked
    pad = rows - block
    if pad:
        left = jnp.pad(left, ((0, 0), (0, pad), (0, 0)))
        left_f = jnp.pad(left_f, ((0, 0), (0, pad)), mode="edge")

    turns = trip_turns[trip]
    operator = jax.vmap(columns_operator, (0, 0, None))
    left_op = operator(rotations[turns[:, 0]], atom_maps[turns[:, 0]], neighbors)
    right_op = operator(rotations[turns[:, 1]], atom_maps[turns[:, 1]], neighbors)
    left_cols = jnp.einsum("ujd,umd->ujm", left, left_op, preferred_element_type=f32)
    left_cols = left_cols.astype(jnp.bfloat16).reshape(units, rows, atoms, width).swapaxes(1, 2)
    right_cols = jnp.einsum("umd,ujd->umj", right_op, right, preferred_element_type=f32)
    right_cols = right_cols.astype(jnp.bfloat16).reshape(units, atoms, width, modes)

    sharp = 1.0 / (2.0 * SMEAR_WIDTH * SMEAR_WIDTH)
    level = (LEVELS + jnp.arange(LEVELS, dtype=f32)) / 512.0
    w1, w2, w0 = left_f.astype(f32), right_f.astype(f32), home_f.astype(f32)
    front = jnp.exp(-sharp * level * level) / (SMEAR_WIDTH * math.sqrt(2.0 * math.pi))
    u1 = front * jnp.exp(2.0 * sharp * w1[:, :, None] * level)
    v1 = front * jnp.exp(-2.0 * sharp * w1[:, :, None] * level)
    u2 = jnp.exp(2.0 * sharp * w2[:, :, None] * level)
    v2 = jnp.exp(-2.0 * sharp * w2[:, :, None] * level)
    w1g = w1.reshape(units, groups, 1, GROUP)
    w2g = w2[:, None, :, None]
    occ1, occ2 = occupation(w1g), occupation(w2g)
    at = (occ1 + occ2 + 1.0) * jnp.exp(-sharp * (w1g + w2g) ** 2) / (w1g * w2g)
    bt = (occ1 - occ2) * jnp.exp(-sharp * (w1g - w2g) ** 2) / (w1g * w2g)

    def spec(shape):
        return pl.BlockSpec((1,) + shape, lambda u: (u,) + (0,) * len(shape))

    n_cols = GROUP * modes
    sums = pl.pallas_call(
        unit_kernel,
        grid=(units,),
        in_specs=[
            spec((atoms, rows, width)),
            spec((atoms, width, modes)),
            pl.BlockSpec((atoms, 3 * width, width), lambda u: (0, 0, 0)),
            spec((modes, comps)),
            spec((groups, modes, GROUP)),
            spec((groups, modes, GROUP)),
            spec((rows, LEVELS)),
            spec((rows, LEVELS)),
            spec((modes, LEVELS)),
            spec((modes, LEVELS)),
        ],
        out_specs=spec((modes, 2 * LEVELS)),
        out_shape=jax.ShapeDtypeStruct((units, modes, 2 * LEVELS), f32),
        scratch_shapes=[
            pltpu.VMEM((atoms, width, 768), jnp.bfloat16),
            pltpu.VMEM((atoms, width, 128), jnp.bfloat16),
            pltpu.VMEM((rows * comps, 128), f32),
            pltpu.VMEM((rows * comps, 128), f32),
            pltpu.VMEM((rows * atoms, 128), f32),
            pltpu.VMEM((modes, n_cols), jnp.bfloat16),
            pltpu.VMEM((n_cols, 2 * LEVELS), jnp.bfloat16),
        ],
        compiler_params=pltpu.CompilerParams(vmem_limit_bytes=60 * 1024 * 1024),
    )(
        left_cols, right_cols, force_consts.reshape(atoms, 3 * width, width),
        jnp.concatenate([home[:, :, x::3] for x in range(3)], axis=2),
        at, bt, u1, v1, u2, v2,
    )
    folded = sums[:, :, :LEVELS] + sums[:, :, LEVELS:]
    mine = jnp.where(w0[:, :, None] == level, folded, 0.0)
    prefactor = 16.0 / (modes * modes)
    rates = jnp.sum(mine, axis=2) * (trip_weights[trip].astype(f32) * prefactor)[:, None] / w0
    hits = (jnp.arange(pb_count, dtype=jnp.int32)[:, None] == owner[None, :]).astype(f32)
    lines = jnp.sum(hits[:, :, None] * rates[None], axis=1)
    total = lax.psum(lines, ("pb", "fc", "br"))
    return lax.dynamic_slice_in_dim(total, lax.axis_index("pb"), 1, 0)


def solution(mesh):
    return jax.shard_map(
        shards,
        mesh=mesh,
        in_specs=(
            P(("groups", "pb"), "br", None),
            P(("groups", "pb"), "br"),
            P(),
            P(),
            P(),
            P(),
            P("groups"),
            P("groups", None),
            P("groups", None),
            P("groups"),
        ),
        out_specs=P(("groups", "pb"), None),
        check_vma=False,
    )
```

profile of v0, /device:TPU:0, one launch (start us, length us, event | category | flops | bytes accessed | tf_op | source)
XLA Modules:
  0.0 383.5 jit_solution(13584231661954305485)
XLA Ops:
  13.6 1.6 constant_dynamic-slice_fusion.21
  37.0 1.6 gather_fusion.2
  39.4 1.6 gather_fusion.5
  42.0 1.3 broadcast_compare_fusion
  43.3 5.9 %select_convert_fusion = bf16[3,96,8,3,288]{4,3,2,1,0:T(4,128)(2,1)} fusion(s32[3,3,288]{2,1,0:T(4,128)S(1)} %tile.21, pred[3,96,8,288]{3,2,1,0:T(8,128)(4,1)S(1)} %get-tuple-element.37), kind=kLoop, calls=%fused_computation.8 | loop fusion | flops 3981312 | bytes 4655232 | tf_op jit(solution)/shard_map/vmap()/convert_element_type | solution.py:26
  49.1 13.7 %convert_element_type.92 = bf16[3,2304,288]{2,1,0:T(8,128)(2,1)} reshape(bf16[3,96,8,3,288]{4,3,2,1,0:T(4,128)(2,1)} %select_convert_fusion) | data formatting | bytes 7962624 | tf_op jit(solution)/shard_map/vmap()/convert_element_type | solution.py:26
  63.2 5.9 %select_convert_fusion.1 = bf16[3,96,8,3,288]{4,3,2,1,0:T(4,128)(2,1)} fusion(s32[3,3,288]{2,1,0:T(4,128)S(1)} %tile.9, pred[3,96,8,288]{3,2,1,0:T(8,128)(4,1)S(1)} %get-tuple-element.38), kind=kLoop, calls=%fused_computation.9 | loop fusion | flops 3981312 | bytes 4655232 | tf_op jit(solution)/shard_map/vmap()/convert_element_type | solution.py:26
  69.1 13.8 %convert_element_type.89 = bf16[3,2304,288]{2,1,0:T(8,128)(2,1)} reshape(bf16[3,96,8,3,288]{4,3,2,1,0:T(4,128)(2,1)} %select_convert_fusion.1) | data formatting | bytes 7962624 | tf_op jit(solution)/shard_map/vmap()/convert_element_type | solution.py:26
  82.9 15.6 %all-gather = bf16[8,4,288]{2,1,0:T(4,128)(2,1)S(1)} all-gather(bf16[1,4,288]{2,1,0:T(4,128)(2,1)S(1)} %bitcast.41), channel_id=1, replica_groups=mesh['groups'=2,'pb'=8,'fc'=2,'br'=1] {'pb'}, dimensions={0}, use_global_device_ids=true | all-gather | bytes 20736 | tf_op jit(solution)/shard_map/all_gather | solution.py:138
  104.2 2.5 copy.79.forces_ref
  110.4 1.3 multiply_exponential_fusion
  111.7 4.7 %multiply_divide_fusion = (f32[3,9,288,8]{3,2,1,0:T(8,128)}, f32[3,9,288,8]{3,2,1,0:T(8,128)}) fusion(f32[3,288]{1,0:T(4,128)S(1)} %fusion.26, f32[3,9,8]{2,1,0:T(8,128)S(1)} %maximum_convert_fusion, f32[3,288]{1,0:T(4,128)S(1)} %get-tuple-element.36, f32[3,9,8]{2,1,0:T(8,128)S(1)} %exponential-minus-one_divide_fusion), kind=kLoop, calls=%fused_computation.10 | loop fusion | flops 870912 | bytes 506304 | tf_op jit(solution)/shard_map/div | solution.py:188
  116.4 1.5 constant_dynamic-slice_fusion.6
  118.1 7.1 %slice.67 = bf16[3,288,96]{2,1,0:T(8,128)(2,1)S(1)} slice(bf16[3,288,288]{2,1,0:T(8,128)(2,1)S(1)} %pad_maximum_fusion), slice={[0:3:1], [0:288:1], [0:288:3]} | slice | bytes 331776 | tf_op jit(solution)/shard_map/slice | solution.py:223
  125.2 7.3 %slice.68 = bf16[3,288,96]{2,1,0:T(8,128)(2,1)S(1)} slice(bf16[3,288,288]{2,1,0:T(8,128)(2,1)S(1)} %pad_maximum_fusion), slice={[0:3:1], [0:288:1], [1:288:3]} | slice | bytes 331776 | tf_op jit(solution)/shard_map/slice | solution.py:223
  132.5 7.2 %slice.69 = bf16[3,288,96]{2,1,0:T(8,128)(2,1)S(1)} slice(bf16[3,288,288]{2,1,0:T(8,128)(2,1)S(1)} %pad_maximum_fusion), slice={[0:3:1], [0:288:1], [2:288:3]} | slice | bytes 331776 | tf_op jit(solution)/shard_map/slice | solution.py:223
  139.7 6.7 %convolution_convert_fusion = bf16[3,2304,288]{1,2,0:T(8,128)(2,1)} fusion(bf16[3,2304,288]{2,1,0:T(8,128)(2,1)} %convert_element_type.92, bf16[1,288,288]{2,1,0:T(8,128)(2,1)S(1)} %get-tuple-element.16, bf16[1,288,288]{2,1,0:T(8,128)(2,1)S(1)} %get-tuple-element.17, bf16[1,288,288]{2,1,0:T(8,128)(2,1)S(1)} %get-tuple-element.18), kind=kOutput, calls=%fused_computation.12 | convolution fusion | flops 1149106176 | bytes 8460288 | tf_op jit(solution)/shard_map/umd,ujd->umj/dot_general | solution.py:173
  146.4 6.6 %copy.77 = bf16[3,2304,288]{2,1,0:T(8,128)(2,1)} copy(bf16[3,2304,288]{1,2,0:T(8,128)(2,1)} %convolution_convert_fusion) | data formatting | bytes 7962624 | tf_op jit(solution)/shard_map/convert_element_type | solution.py:174
  154.0 4.2 %convolution_convert_fusion.1 = bf16[3,72,2304]{2,1,0:T(8,128)(2,1)S(1)} fusion(bf16[3,2304,288]{2,1,0:T(8,128)(2,1)} %convert_element_type.89, bf16[1,72,288]{2,1,0:T(8,128)(2,1)S(1)} %get-tuple-element.20, bf16[1,72,288]{2,1,0:T(8,128)(2,1)S(1)} %get-tuple-element.21, bf16[1,72,288]{2,1,0:T(8,128)(2,1)S(1)} %get-tuple-element.19), kind=kOutput, calls=%fused_computation.13 | convolution fusion | flops 287276544 | bytes 5101056 | tf_op jit(solution)/shard_map/ujd,umd->ujm/dot_general | solution.py:171
  159.3 4.5 %copy.72 = bf16[3,72,96,24]{3,1,2,0:T(8,128)(2,1)} copy(bf16[3,72,96,24]{1,3,2,0:T(8,128)(2,1)S(1)} %bitcast.37) | data formatting | bytes 1990656 | tf_op jit(solution)/shard_map/reshape | solution.py:172
  163.8 1.2 pad_maximum_fusion.1.home_ref
  165.0 147.6 %shard_map.100 = f32[3,288,256]{2,1,0:T(8,128)} custom-call(bf16[3,96,72,24]{3,2,1,0:T(8,128)(2,1)} %bitcast.36, bf16[3,96,24,288]{3,2,1,0:T(8,128)(2,1)} %bitcast.35, bf16[96,72,24]{2,1,0:T(8,128)(2,1)} %copy.79.forces_ref, bf16[3,288,288]{2,1,0:T(8,128)(2,1)} %pad_maximum_fusion.1.home_ref, f32[3,9,288,8]{3,2,1,0:T(8,128)} %get-tuple-element.23.at_ref, ...), custom_call_target="tpu_custom_call" | custom-call | tf_op jit(solution)/shard_map/pallas_call | solution.py:194
  312.6 1.5 fusion.6
  314.3 61.7 %psum.7 = f32[8,288]{1,0:T(8,128)S(1)} all-reduce(f32[8,288]{1,0:T(8,128)S(1)} %multiply_reduce_fusion), channel_id=1, replica_groups=mesh['groups'=2,'pb'=8,'fc'=2,'br'=1] {'pb','fc','br'}, use_global_device_ids=true, to_apply=%region_4.5 | all-reduce | flops 2304 | bytes 18432 | tf_op jit(solution)/shard_map/psum | solution.py:232
  (71 shorter events, 18.7 us)
Async XLA Ops:
  6.5 26.4 %copy-start = (s32[48,96]{1,0:T(8,128)S(1)}, s32[48,96]{1,0:T(8,128)}, u32[]{:S(2)}) copy-start(s32[48,96]{1,0:T(8,128)} %param.15) | copy-start | bytes 55300
  6.5 109.8 %all-gather.3.cloned.1.call-start = ((), (), s32[]{:S(2)}) async-start(), calls=%async_computation | async-start | bytes 7962624 | tf_op jit(solution)/shard_map/all_gather | solution.py:137
  69.1 13.8 %copy-start.4 = (bf16[4,288]{1,0:T(4,128)(2,1)S(1)}, bf16[4,288]{1,0:T(4,128)(2,1)}, u32[]{:S(2)}) copy-start(bf16[4,288]{1,0:T(4,128)(2,1)} %param.11) | copy-start | bytes 6916
  69.1 34.9 %copy-start.3 = (bf16[96,3,576]{2,0,1:T(8,128)(2,1)S(1)}, bf16[96,3,576]{2,0,1:T(8,128)(2,1)}, u32[]{:S(2)}) copy-start(bf16[96,3,576]{2,0,1:T(8,128)(2,1)} %param.12) | copy-start | bytes 995332
  69.1 37.7 %copy-start.2 = (s32[12]{0:T(128)S(1)}, s32[12]{0:T(128)}, u32[]{:S(2)}) copy-start(s32[12]{0:T(128)} %param.19) | copy-start | bytes 148
  165.0 211.6 %copy-start.1 = (s32[48,96]{1,0:T(8,128)S(1)}, s32[48,96]{1,0:T(8,128)}, u32[]{:S(2)}) copy-start(s32[48,96]{1,0:T(8,128)} %param.15) | copy-start | bytes 55300
Sparse Core Ops, SparseCore 0:
  9.0 73.9 all-gather.2
where the time goes:
time: 385 us; the launch traced here: 383 us
  Pallas kernels  148 us (38%)
  local copies, waits for them, and re-layouts  83 us (22%)
  blocking collectives  77.3 us (20%)
  between operations  38.2 us (10%)
  other arithmetic  25.7 us (7%)
  matrix products  10.9 us (3%)
    pallas_call x1, Pallas kernels, shards(): pl.pallas_call(unit_kernel, grid=(units,), in_specs=[spec((atoms, rows, w...  148 us
    psum x1, blocking collectives, shards(): total = lax.psum(lines, ('pb', 'fc', 'br'))  61.7 us
    convert_element_type x2, local copies, waits for them, and re-layouts, columns_operator(): return rows.astype(jnp.bfloat16).reshape(3 * atoms * slots, 3 * atoms)  27.5 us
    slice x3, local copies, waits for them, and re-layouts, shards(): home[:, :, x::3]  21.6 us
    all_gather x1, blocking collectives, shards(): freq_table = lax.all_gather(frequencies, 'pb', axis=0, tiled=True)  15.6 us
    convert_element_type x2, other arithmetic, columns_operator(): return rows.astype(jnp.bfloat16).reshape(3 * atoms * slots, 3 * atoms)  11.7 us
  transfers between devices with their start and end apart: 1, of which 0 were waited for; matrix products, arithmetic and copies ran while one was open for 18% of the time, Pallas kernels for 0%

commit v1 on v0

--- a/solution.py
+++ b/solution.py
@@ -18,12 +18,32 @@
 
 def columns_operator(turned, mapping, neighbors):
     atoms, slots = neighbors.shape
-    target = mapping[neighbors]
+    axis = jnp.sum(jnp.abs(turned) * jnp.arange(3, dtype=jnp.int32), axis=1)
+    sign = jnp.sum(turned, axis=1)
+    target = mapping[neighbors.reshape(-1)]
+    column = (target[:, None] * 3 + axis[None, :]).reshape(-1)
+    signs = jnp.tile(sign, atoms * slots).astype(jnp.float32)
     comp = jnp.arange(3 * atoms, dtype=jnp.int32)
-    hit = target[:, :, None, None] == (comp // 3)[None, None, None, :]
-    axes = jnp.tile(turned, (1, atoms))
-    rows = jnp.where(hit, axes[None, None, :, :], 0)
-    return rows.astype(jnp.bfloat16).reshape(3 * atoms * slots, 3 * atoms)
+    return jnp.where(column[:, None] == comp[None, :], signs[:, None], 0.0).astype(jnp.bfloat16)
+
+
+def exchange_sums(lines):
+    for name in ("fc", "br"):
+        hop = lax.axis_size(name) // 2
+        while hop:
+            pairs = [(i, i ^ hop) for i in range(lax.axis_size(name))]
+            lines = lines + lax.ppermute(lines, name, pairs)
+            hop //= 2
+    place = lax.axis_index("pb")
+    hop = lax.axis_size("pb") // 2
+    while hop:
+        pairs = [(i, i ^ hop) for i in range(lax.axis_size("pb"))]
+        upper = (place & hop) != 0
+        low, high = lines[:hop], lines[hop:]
+        given = lax.ppermute(jnp.where(upper, low, high), "pb", pairs)
+        lines = jnp.where(upper, high, low) + given
+        hop //= 2
+    return lines
 
 
 def unit_kernel(
@@ -134,11 +154,12 @@
     groups = rows // GROUP
     f32 = jnp.float32
 
-    table = lax.all_gather(eigen_vectors, "pb", axis=0, tiled=True)
-    freq_table = lax.all_gather(frequencies, "pb", axis=0, tiled=True)
     if br_count > 1:
-        table = lax.all_gather(table, "br", axis=1, tiled=True)
-        freq_table = lax.all_gather(freq_table, "br", axis=1, tiled=True)
+        eigen_vectors = lax.all_gather(eigen_vectors, "br", axis=1, tiled=True)
+        frequencies = lax.all_gather(frequencies, "br", axis=1, tiled=True)
+    table = lax.all_gather(
+        jnp.concatenate([eigen_vectors, frequencies[:, None, :]], axis=1), "pb", axis=0, tiled=True
+    )
 
     starts = jnp.cumsum(grid_counts) - grid_counts
     ids = me * units + jnp.arange(units, dtype=jnp.int32)
@@ -150,11 +171,11 @@
         t = trip[u]
         left_q, right_q = trip_partners[t, 0], trip_partners[t, 1]
         left = lax.dynamic_slice(table, (left_q, first[u], 0), (1, block, comps))[0]
-        left_f = lax.dynamic_slice(freq_table, (left_q, first[u]), (1, block))[0]
-        home = lax.dynamic_index_in_dim(table, owner[u] * held, 0, False)
-        home_f = lax.dynamic_index_in_dim(freq_table, owner[u] * held, 0, False)
-        right = lax.dynamic_index_in_dim(table, right_q, 0, False)
-        right_f = lax.dynamic_index_in_dim(freq_table, right_q, 0, False)
+        left_f = lax.dynamic_slice(table, (left_q, modes, first[u]), (1, 1, block))[0, 0]
+        home = lax.dynamic_slice(table, (owner[u] * held, 0, 0), (1, modes, comps))[0]
+        home_f = lax.dynamic_slice(table, (owner[u] * held, modes, 0), (1, 1, modes))[0, 0]
+        right = lax.dynamic_slice(table, (right_q, 0, 0), (1, modes, comps))[0]
+        right_f = lax.dynamic_slice(table, (right_q, modes, 0), (1, 1, modes))[0, 0]
         return left, left_f, home, home_f, right, right_f
 
     picked = [jnp.stack(p) for p in zip(*[rows_of(u) for u in range(units)])]
@@ -163,6 +184,11 @@
     if pad:
         left = jnp.pad(left, ((0, 0), (0, pad), (0, 0)))
         left_f = jnp.pad(left_f, ((0, 0), (0, pad)), mode="edge")
+
+    comp = jnp.arange(comps, dtype=jnp.int32)
+    order = comp[:, None] == (comp % atoms * 3 + comp // atoms)[None, :]
+    home = jnp.einsum("ujc,cd->ujd", home, order.astype(jnp.bfloat16), preferred_element_type=f32)
+    home = home.astype(jnp.bfloat16)
 
     turns = trip_turns[trip]
     operator = jax.vmap(columns_operator, (0, 0, None))
@@ -220,7 +246,7 @@
         compiler_params=pltpu.CompilerParams(vmem_limit_bytes=60 * 1024 * 1024),
     )(
         left_cols, right_cols, force_consts.reshape(atoms, 3 * width, width),
-        jnp.concatenate([home[:, :, x::3] for x in range(3)], axis=2),
+        home,
         at, bt, u1, v1, u2, v2,
     )
     folded = sums[:, :, :LEVELS] + sums[:, :, LEVELS:]
@@ -229,8 +255,7 @@
     rates = jnp.sum(mine, axis=2) * (trip_weights[trip].astype(f32) * prefactor)[:, None] / w0
     hits = (jnp.arange(pb_count, dtype=jnp.int32)[:, None] == owner[None, :]).astype(f32)
     lines = jnp.sum(hits[:, :, None] * rates[None], axis=1)
-    total = lax.psum(lines, ("pb", "fc", "br"))
-    return lax.dynamic_slice_in_dim(total, lax.axis_index("pb"), 1, 0)
+    return exchange_sums(lines)
 
 
 def solution(mesh):

time: 385 us -> 288 us (0.75)
  blocking collectives: 77.3 us -> 0 us
  local copies, waits for them, and re-layouts: 83 us -> 37.7 us
  waiting for transfers between devices: 0.71 us -> 37.2 us
  other arithmetic: 25.7 us -> 12.1 us
  between operations: 38.2 us -> 43 us
  matrix products: 10.9 us -> 6.49 us
    psum x1 -> x0, blocking collectives: 61.7 us -> none  [shards(): total = lax.psum(lines, ('pb', 'fc', 'br'))]
    all_gather x1, waiting for transfers between devices: 0.01 us -> 26.8 us  [shards(): lax.all_gather(jnp.concatenate([eigen_vectors, frequencies[:, None, :]],...]
    convert_element_type x2, local copies, waits for them, and re-layouts: 27.5 us -> 1.56 us  [columns_operator(): signs = jnp.tile(sign, atoms * slots).astype(jnp.float32)]
    slice x4 -> x1, local copies, waits for them, and re-layouts: 22.2 us -> 0.65 us  [rows_of(): owner[u] * held]
    all_gather x1 -> x0, blocking collectives: 15.6 us -> none  [shards(): freq_table = lax.all_gather(frequencies, 'pb', axis=0, tiled=True)]
    convert_element_type x2, other arithmetic: 11.7 us -> 0.01 us  [columns_operator(): signs = jnp.tile(sign, atoms * slots).astype(jnp.float32)]
    ppermute x0 -> x4, waiting for transfers between devices: none -> 10.4 us  [the longest x3 8.2 us: exchange_sums(): given = lax.ppermute(jnp.where(upper, low, high), 'pb', pairs)]
  transfers between devices with their start and end apart: 1 -> 5, of which waited for: 0 -> 5; matrix products, arithmetic and copies ran while one was open for 18% -> 6% of each run, Pallas kernels for 0% -> 0%
where the time goes in v1:
time: 288 us; the launch traced here: 287 us
  Pallas kernels  148 us (51%)
  between operations  43 us (15%)
  local copies, waits for them, and re-layouts  37.7 us (13%)
  waiting for transfers between devices  37.2 us (13%)
  other arithmetic  12.1 us (4%)
  matrix products  6.49 us (2%)
    pallas_call x1, Pallas kernels, shards(): pl.pallas_call(unit_kernel, grid=(units,), in_specs=[spec((atoms, rows, w...  148 us
    all_gather x1, waiting for transfers between devices, shards(): lax.all_gather(jnp.concatenate([eigen_vectors, frequencies[:, None, :]],...  26.8 us
    ppermute x3, waiting for transfers between devices, exchange_sums(): given = lax.ppermute(jnp.where(upper, low, high), 'pb', pairs)  8.2 us
    convert_element_type x1, local copies, waits for them, and re-layouts, shards(): right_cols.astype(jnp.bfloat16).reshape(units, atoms, width, modes)  6.56 us
  transfers between devices with their start and end apart: 5, of which 5 were waited for; matrix products, arithmetic and copies ran while one was open for 6% of the time, Pallas kernels for 0%

profile of v1, /device:TPU:0, one launch (start us, length us, event | category | flops | bytes accessed | tf_op | source)
XLA Modules:
  0.0 286.9 jit_solution(14215748324361148621)
XLA Ops:
  7.5 1.6 copy.104
  9.1 1.1 pad_maximum_fusion
  39.6 1.6 gather_fusion.2
  43.4 1.6 gather_fusion.5
  46.5 2.4 copy.127.forces_ref
  57.5 26.8 %all-gather.2.cloned.1.call-done = bf16[32,289,288]{1,2,0:T(8,128)(2,1)} async-done(((bf16[4,289,288]{1,2,0:T(8,128)(2,1)}), bf16[32,289,288]{1,2,0:T(8,128)(2,1)}) %all-gather.2.cloned.1.call-update) | async-done | bytes 5326864 | tf_op jit(solution)/shard_map/all_gather | solution.py:160
  84.3 1.5 dynamic-slice_reduce_fusion.5
  87.3 1.2 constant_dynamic-slice_fusion.10
  89.7 1.1 copy.114
  90.9 4.5 %copy.115 = bf16[3,72,96,24]{3,1,2,0:T(8,128)(2,1)} copy(bf16[3,72,96,24]{1,3,2,0:T(8,128)(2,1)S(1)} %bitcast.35) | data formatting | bytes 1990656 | tf_op jit(solution)/shard_map/reshape | solution.py:198
  95.4 1.5 constant_dynamic-slice_fusion.2
  97.5 4.1 %convolution_convert_fusion = bf16[3,2304,288]{1,2,0:T(8,128)(2,1)} fusion(bf16[3,2304]{1,0:T(4,128)(2,1)S(1)} %convert_element_type.111, s32[3,2304]{1,0:T(4,128)S(1)} %add.309, bf16[1,288,288]{2,1,0:T(8,128)(2,1)S(1)} %copy.133, bf16[1,288,288]{2,1,0:T(8,128)(2,1)S(1)} %copy.132, bf16[1,288,288]{2,1,0:T(8,128)(2,1)S(1)} %copy.131), kind=kOutput, calls=%fused_computation.14 | convolution fusion | flops 1154082816 | bytes 4520448 | tf_op jit(solution)/shard_map/umd,ujd->umj/dot_general | solution.py:199
  101.7 6.6 %copy.122 = bf16[3,2304,288]{2,1,0:T(8,128)(2,1)} copy(bf16[3,2304,288]{1,2,0:T(8,128)(2,1)} %convolution_convert_fusion) | data formatting | bytes 7962624 | tf_op jit(solution)/shard_map/convert_element_type | solution.py:200
  108.8 1.3 multiply_exponential_fusion
  110.9 1.4 convolution_convert_fusion.1.home_ref
  112.4 4.6 %multiply_divide_fusion = (f32[3,9,288,8]{3,2,1,0:T(8,128)}, f32[3,9,288,8]{3,2,1,0:T(8,128)}) fusion(f32[3,288]{1,0:T(4,128)S(1)} %fusion.53, f32[3,9,8]{2,1,0:T(8,128)S(1)} %maximum_convert_fusion, f32[3,288]{1,0:T(4,128)S(1)} %get-tuple-element.33, f32[3,9,8]{2,1,0:T(8,128)S(1)} %exponential-minus-one_divide_fusion), kind=kLoop, calls=%fused_computation.12 | loop fusion | flops 870912 | bytes 506304 | tf_op jit(solution)/shard_map/div | solution.py:214
  117.0 147.6 %shard_map.100 = f32[3,288,256]{2,1,0:T(8,128)} custom-call(bf16[3,96,72,24]{3,2,1,0:T(8,128)(2,1)} %bitcast.33, bf16[3,96,24,288]{3,2,1,0:T(8,128)(2,1)} %bitcast.34, bf16[96,72,24]{2,1,0:T(8,128)(2,1)} %copy.127.forces_ref, bf16[3,288,288]{2,1,0:T(8,128)(2,1)} %convolution_convert_fusion.1.home_ref, f32[3,9,288,8]{3,2,1,0:T(8,128)} %get-tuple-element.30.at_ref, ...), custom_call_target="tpu_custom_call" | custom-call | tf_op jit(solution)/shard_map/pallas_call | solution.py:220
  264.6 1.5 fusion.19
  266.3 1.5 collective-permute-start
  267.7 2.2 collective-permute-done
  270.0 1.1 collective-permute-start.1
  271.1 3.5 %collective-permute-done.1 = f32[4,288]{1,0:T(4,128)S(1)} collective-permute-done((f32[4,288]{1,0:T(4,128)S(1)}, f32[4,288]{1,0:T(4,128)S(1)}, u32[]{:S(2)}, u32[]{:S(2)}) %collective-permute-start.1) | collective-permute-done | bytes 4640 | tf_op jit(solution)/shard_map/ppermute | solution.py:43
  274.7 3.6 %collective-permute-done.2 = f32[2,288]{1,0:T(2,128)S(1)} collective-permute-done((f32[2,288]{1,0:T(2,128)S(1)}, f32[2,288]{1,0:T(2,128)S(1)}, u32[]{:S(2)}, u32[]{:S(2)}) %collective-permute-start.2) | collective-permute-done | bytes 2336 | tf_op jit(solution)/shard_map/ppermute | solution.py:43
  278.3 1.1 collective-permute-done.3
  (106 shorter events, 18.9 us)
Async XLA Ops:
  6.5 21.6 %copy-start = (s32[48,96]{1,0:T(8,128)S(1)}, s32[48,96]{1,0:T(8,128)}, u32[]{:S(2)}) copy-start(s32[48,96]{1,0:T(8,128)} %param.15) | copy-start | bytes 55300
  6.5 10.3 %copy-start.3 = (s32[12,2]{0,1:T(2,128)S(1)}, s32[12,2]{0,1:T(2,128)}, u32[]{:S(2)}) copy-start(s32[12,2]{0,1:T(2,128)} %param.17) | copy-start | bytes 292
  6.5 19.3 %copy-start.4 = (s32[48,3,3]{0,2,1:T(4,128)S(1)}, s32[48,3,3]{0,2,1:T(4,128)}, u32[]{:S(2)}) copy-start(s32[48,3,3]{0,2,1:T(4,128)} %param.14) | copy-start | bytes 5188
  6.5 19.5 %copy-start.6 = (s32[12,2]{0,1:T(2,128)S(1)}, s32[12,2]{0,1:T(2,128)}, u32[]{:S(2)}) copy-start(s32[12,2]{0,1:T(2,128)} %param.18) | copy-start | bytes 292
  6.5 22.7 %copy-start.7 = (s32[8]{0:T(128)S(1)}, s32[8]{0:T(128)}, u32[]{:S(2)}) copy-start(s32[8]{0:T(128)} %param.16) | copy-start | bytes 100
  6.5 32.8 %copy-start.5 = (s32[96,8]{0,1:T(8,128)S(1)}, s32[96,8]{0,1:T(8,128)}, u32[]{:S(2)}) copy-start(s32[96,8]{0,1:T(8,128)} %param.13) | copy-start | bytes 9220
  6.6 77.8 %all-gather.2.cloned.1.call-start = ((), (), s32[]{:S(2)}) async-start(), calls=%async_computation | async-start | bytes 7962624 | tf_op jit(solution)/shard_map/all_gather | solution.py:160
  41.2 5.0 %copy-start.2 = (bf16[96,3,576]{2,0,1:T(8,128)(2,1)S(1)}, bf16[96,3,576]{2,0,1:T(8,128)(2,1)}, u32[]{:S(2)}) copy-start(bf16[96,3,576]{2,0,1:T(8,128)(2,1)} %param.12) | copy-start | bytes 995332
  42.5 10.5 %copy-start.1 = (s32[12]{0:T(128)S(1)}, s32[12]{0:T(128)}, u32[]{:S(2)}) copy-start(s32[12]{0:T(128)} %param.19) | copy-start | bytes 148
  266.3 3.7 %collective-permute-start = (f32[8,288]{1,0:T(8,128)S(1)}, f32[8,288]{1,0:T(8,128)S(1)}, u32[]{:S(2)}, u32[]{:S(2)}) collective-permute-start(f32[8,288]{1,0:T(8,128)S(1)} %multiply_reduce_fusion), channel_id=1, source_target_pairs={{0,1},{1,0},{2,3},{3,2},{4,5},{5,4},{6,7},{7,6},{8,9},{9,8},{10,11... | collective-permute-start | bytes 27656 | tf_op jit(solution)/shard_map/ppermute | solution.py:35
  270.0 4.6 %collective-permute-start.1 = (f32[4,288]{1,0:T(4,128)S(1)}, f32[4,288]{1,0:T(4,128)S(1)}, u32[]{:S(2)}, u32[]{:S(2)}) collective-permute-start(f32[4,288]{1,0:T(4,128)S(1)} %slice_select_fusion), channel_id=1, source_target_pairs={{0,8},{2,10},{4,12},{6,14},{8,0},{10,2},{12,4},{14,6},{1,9},{3,11}... | collective-permute-start | bytes 13832 | tf_op jit(solution)/shard_map/ppermute | solution.py:43
  274.6 3.7 %collective-permute-start.2 = (f32[2,288]{1,0:T(2,128)S(1)}, f32[2,288]{1,0:T(2,128)S(1)}, u32[]{:S(2)}, u32[]{:S(2)}) collective-permute-start(f32[2,288]{1,0:T(2,128)S(1)} %broadcast_select_fusion), channel_id=1, source_target_pairs={{0,4},{2,6},{4,0},{6,2},{8,12},{10,14},{12,8},{14,10},{1,5},{3,7},... | collective-permute-start | bytes 6920 | tf_op jit(solution)/shard_map/ppermute | solution.py:43
  278.3 1.2 collective-permute-start.3
Sparse Core Ops, SparseCore 0:
  10.3 73.9 all-gather.1

commit v2 on v1

--- a/solution.py
+++ b/solution.py
@@ -56,9 +56,10 @@
     tail = modes - 256
 
     def halves(step, _):
-        for inner in range(8):
-            a = step * 8 + inner
-            h = jnp.dot(forces_ref[a], right_ref[0, a], preferred_element_type=jnp.float32)
+        for inner in range(16):
+            a = step * 16 + inner
+            right = right_ref[0, a].astype(jnp.bfloat16)
+            h = jnp.dot(forces_ref[a], right, preferred_element_type=jnp.float32)
             parts = [h[x * width : (x + 1) * width] for x in range(3)]
             half_main[a] = jnp.concatenate([p[:, :256] for p in parts], axis=1).astype(jnp.bfloat16)
             ends = [p[:, 256:] for p in parts]
@@ -66,11 +67,11 @@
             half_tail[a] = jnp.concatenate(ends, axis=1).astype(jnp.bfloat16)
         return 0
 
-    lax.fori_loop(0, atoms // 8, halves, 0)
+    lax.fori_loop(0, atoms // 16, halves, 0)
 
     def reduce_atoms(step, _):
-        for inner in range(8):
-            a = step * 8 + inner
+        for inner in range(16):
+            a = step * 16 + inner
             left = left_ref[0, a]
             main = jnp.dot(left, half_main[a], preferred_element_type=jnp.float32)
             ends = jnp.dot(left, half_tail[a], preferred_element_type=jnp.float32)
@@ -81,7 +82,7 @@
             red_tail[pl.ds(a, rows, stride=atoms), :] = ends
         return 0
 
-    lax.fori_loop(0, atoms // 8, reduce_atoms, 0)
+    lax.fori_loop(0, atoms // 16, reduce_atoms, 0)
 
     def weigh(spot, a_col, b_col, u1, v1, u2, v2):
         q = u1 * (a_col * u2 - b_col * v2) + v1 * (b_col * u2 - a_col * v2)
@@ -197,7 +198,7 @@
     left_cols = jnp.einsum("ujd,umd->ujm", left, left_op, preferred_element_type=f32)
     left_cols = left_cols.astype(jnp.bfloat16).reshape(units, rows, atoms, width).swapaxes(1, 2)
     right_cols = jnp.einsum("umd,ujd->umj", right_op, right, preferred_element_type=f32)
-    right_cols = right_cols.astype(jnp.bfloat16).reshape(units, atoms, width, modes)
+    right_cols = right_cols.reshape(units, atoms, width, modes)
 
     sharp = 1.0 / (2.0 * SMEAR_WIDTH * SMEAR_WIDTH)
     level = (LEVELS + jnp.arange(LEVELS, dtype=f32)) / 512.0

time: 288 us -> 283 us (0.983)
  Pallas kernels: 148 us -> 143 us
  other arithmetic: 12.1 us -> 15.8 us
  local copies, waits for them, and re-layouts: 37.7 us -> 34.7 us
    convert_element_type x1 -> x0, local copies, waits for them, and re-layouts: 6.56 us -> none  [shards(): right_cols.astype(jnp.bfloat16).reshape(units, atoms, width, modes)]
    pallas_call x1, Pallas kernels: 148 us -> 143 us  [shards(): pl.pallas_call(unit_kernel, grid=(units,), in_specs=[spec((atoms, rows, w...]
    unnamed x30 -> x70, local copies, waits for them, and re-layouts: 3.58 us -> 6.13 us
  transfers between devices with their start and end apart: 5 -> 5, of which waited for: 5 -> 5; matrix products, arithmetic and copies ran while one was open for 6% -> 8% of each run, Pallas kernels for 0% -> 0%
where the time goes in v2:
time: 283 us
  Pallas kernels  143 us (51%)
  between operations  41.6 us (15%)
  waiting for transfers between devices  35.5 us (13%)
  local copies, waits for them, and re-layouts  34.7 us (12%)
  other arithmetic  15.8 us (6%)
  matrix products  9.18 us (3%)
    pallas_call x1, Pallas kernels, shards(): pl.pallas_call(unit_kernel, grid=(units,), in_specs=[spec((atoms, rows, w...  143 us
    all_gather x1, waiting for transfers between devices, shards(): lax.all_gather(jnp.concatenate([eigen_vectors, frequencies[:, None, :]],...  25 us
    ppermute x3, waiting for transfers between devices, exchange_sums(): given = lax.ppermute(jnp.where(upper, low, high), 'pb', pairs)  8.21 us
    dot_general x1, matrix products, shards(): jnp.einsum('umd,ujd->umj', right_op, right, preferred_element_type=f32)  6.81 us
    unnamed x70, local copies, waits for them, and re-layouts  6.13 us
  transfers between devices with their start and end apart: 5, of which 5 were waited for; matrix products, arithmetic and copies ran while one was open for 8% of the time, Pallas kernels for 0%

profile of v2, /device:TPU:0, one launch (start us, length us, event | category | flops | bytes accessed | tf_op | source)
XLA Modules:
  0.0 282.7 jit_solution(3405394524463602321)
XLA Ops:
  6.6 1.6 copy.104
  9.1 1.1 pad_maximum_fusion
  37.4 1.6 gather_fusion.5
  40.6 1.4 convert_element_type.108
  45.6 1.6 gather_fusion.2
  49.6 2.4 copy.127.forces_ref
  59.3 25.0 %all-gather.2.cloned.1.call-done = bf16[32,289,288]{1,2,0:T(8,128)(2,1)} async-done(((bf16[4,289,288]{1,2,0:T(8,128)(2,1)}), bf16[32,289,288]{1,2,0:T(8,128)(2,1)}) %all-gather.2.cloned.1.call-update) | async-done | bytes 5326864 | tf_op jit(solution)/shard_map/all_gather | solution.py:161
  84.3 2.0 dynamic-slice_reduce_fusion.5
  88.9 1.5 constant_dynamic-slice_fusion.2
  93.5 1.2 constant_dynamic-slice_fusion.10
  96.0 1.1 copy.114
  97.2 4.5 %copy.115 = bf16[3,72,96,24]{3,1,2,0:T(8,128)(2,1)} copy(bf16[3,72,96,24]{1,3,2,0:T(8,128)(2,1)S(1)} %bitcast.35) | data formatting | bytes 1990656 | tf_op jit(solution)/shard_map/reshape | solution.py:199
  101.8 1.2 multiply_exponential_fusion
  104.0 4.9 %multiply_divide_fusion = (f32[3,9,288,8]{3,2,1,0:T(8,128)}, f32[3,9,288,8]{3,2,1,0:T(8,128)}) fusion(f32[3,288]{1,0:T(4,128)S(1)} %fusion.54, f32[3,9,8]{2,1,0:T(8,128)S(1)} %maximum_convert_fusion, f32[3,288]{1,0:T(4,128)S(1)} %get-tuple-element.33, f32[3,9,8]{2,1,0:T(8,128)S(1)} %exponential-minus-one_divide_fusion), kind=kLoop, calls=%fused_computation.12 | loop fusion | flops 870912 | bytes 506304 | tf_op jit(solution)/shard_map/div | solution.py:215
  108.9 1.4 convolution_convert_fusion.home_ref
  110.3 6.8 %fusion.1 = f32[3,2304,288]{2,1,0:T(8,128)} fusion(bf16[3,2304]{1,0:T(4,128)(2,1)S(1)} %copy-done.8, s32[3,2304]{1,0:T(4,128)S(1)} %add.309, bf16[1,288,288]{2,1,0:T(8,128)(2,1)S(1)} %copy.134, bf16[1,288,288]{2,1,0:T(8,128)(2,1)S(1)} %copy.133, bf16[1,288,288]{2,1,0:T(8,128)(2,1)S(1)} %copy.132), kind=kOutput, calls=%fused_computation.15 | convolution fusion | flops 1151096832 | bytes 8501760 | tf_op jit(solution)/shard_map/umd,ujd->umj/dot_general | solution.py:200
  117.1 143.3 %shard_map.100 = f32[3,288,256]{2,1,0:T(8,128)} custom-call(bf16[3,96,72,24]{3,2,1,0:T(8,128)(2,1)} %bitcast.33, f32[3,96,24,288]{3,2,1,0:T(8,128)} %bitcast.34, bf16[96,72,24]{2,1,0:T(8,128)(2,1)} %copy.127.forces_ref, bf16[3,288,288]{2,1,0:T(8,128)(2,1)} %convolution_convert_fusion.home_ref, f32[3,9,288,8]{3,2,1,0:T(8,128)} %get-tuple-element.30.at_ref, ...), custom_call_target="tpu_custom_call" | custom-call | tf_op jit(solution)/shard_map/pallas_call | solution.py:221
  260.4 1.5 fusion.20
  262.1 1.5 collective-permute-start
  263.6 2.2 collective-permute-done
  265.8 1.1 collective-permute-start.1
  266.9 3.5 %collective-permute-done.1 = f32[4,288]{1,0:T(4,128)S(1)} collective-permute-done((f32[4,288]{1,0:T(4,128)S(1)}, f32[4,288]{1,0:T(4,128)S(1)}, u32[]{:S(2)}, u32[]{:S(2)}) %collective-permute-start.1) | collective-permute-done | bytes 4640 | tf_op jit(solution)/shard_map/ppermute | solution.py:43
  270.5 3.6 %collective-permute-done.2 = f32[2,288]{1,0:T(2,128)S(1)} collective-permute-done((f32[2,288]{1,0:T(2,128)S(1)}, f32[2,288]{1,0:T(2,128)S(1)}, u32[]{:S(2)}, u32[]{:S(2)}) %collective-permute-start.2) | collective-permute-done | bytes 2336 | tf_op jit(solution)/shard_map/ppermute | solution.py:43
  274.2 1.1 collective-permute-done.3
  (145 shorter events, 23.9 us)
Async XLA Ops:
  6.5 29.4 %copy-start = (s32[48,96]{1,0:T(8,128)S(1)}, s32[48,96]{1,0:T(8,128)}, u32[]{:S(2)}) copy-start(s32[48,96]{1,0:T(8,128)} %param.15) | copy-start | bytes 55300
  6.5 10.2 %copy-start.9 = (s32[12,2]{0,1:T(2,128)S(1)}, s32[12,2]{0,1:T(2,128)}, u32[]{:S(2)}) copy-start(s32[12,2]{0,1:T(2,128)} %param.17) | copy-start | bytes 292
  6.5 14.6 %copy-start.27 = (s32[8]{0:T(128)S(1)}, s32[8]{0:T(128)}, u32[]{:S(2)}) copy-start(s32[8]{0:T(128)} %param.16) | copy-start | bytes 100
  6.5 27.1 %copy-start.24 = (s32[12,2]{0,1:T(2,128)S(1)}, s32[12,2]{0,1:T(2,128)}, u32[]{:S(2)}) copy-start(s32[12,2]{0,1:T(2,128)} %param.18) | copy-start | bytes 292
  6.5 27.2 %copy-start.11 = (s32[48,3,3]{0,2,1:T(4,128)S(1)}, s32[48,3,3]{0,2,1:T(4,128)}, u32[]{:S(2)}) copy-start(s32[48,3,3]{0,2,1:T(4,128)} %param.14) | copy-start | bytes 5188
  6.5 30.6 %copy-start.22 = (s32[96,8]{0,1:T(8,128)S(1)}, s32[96,8]{0,1:T(8,128)}, u32[]{:S(2)}) copy-start(s32[96,8]{0,1:T(8,128)} %param.13) | copy-start | bytes 9220
  6.6 77.8 %all-gather.2.cloned.1.call-start = ((), (), s32[]{:S(2)}) async-start(), calls=%async_computation | async-start | bytes 7962624 | tf_op jit(solution)/shard_map/all_gather | solution.py:161
  39.8 9.5 %copy-start.2 = (bf16[96,3,576]{2,0,1:T(8,128)(2,1)S(1)}, bf16[96,3,576]{2,0,1:T(8,128)(2,1)}, u32[]{:S(2)}) copy-start(bf16[96,3,576]{2,0,1:T(8,128)(2,1)} %param.12) | copy-start | bytes 995332
  45.6 6.4 %copy-start.1 = (s32[12]{0:T(128)S(1)}, s32[12]{0:T(128)}, u32[]{:S(2)}) copy-start(s32[12]{0:T(128)} %param.19) | copy-start | bytes 148
  97.2 5.9 %copy-start.14 = (bf16[72]{0:T(256)(128)(2,1)S(1)}, bf16[72]{0:T(256)(128)(2,1)}, u32[]{:S(2)}) copy-start(bf16[72]{0:T(256)(128)(2,1)} %copy-done.13) | copy-start | bytes 436
  97.2 5.9 %copy-start.16 = (bf16[72]{0:T(256)(128)(2,1)S(1)}, bf16[72]{0:T(256)(128)(2,1)}, u32[]{:S(2)}) copy-start(bf16[72]{0:T(256)(128)(2,1)} %copy-done.15) | copy-start | bytes 436
  97.2 5.9 %copy-start.18 = (bf16[72]{0:T(256)(128)(2,1)S(1)}, bf16[72]{0:T(256)(128)(2,1)}, u32[]{:S(2)}) copy-start(bf16[72]{0:T(256)(128)(2,1)} %copy-done.17) | copy-start | bytes 436
  97.2 5.9 %copy-start.25 = (f32[128]{0:T(128)S(1)}, f32[128]{0:T(128)}, u32[]{:S(2)}) copy-start(f32[128]{0:T(128)} %exponential_multiply_fusion.2) | copy-start | bytes 1540
  104.0 4.9 %copy-start.3 = (bf16[1,288,288]{2,1,0:T(8,128)(2,1)S(1)}, bf16[1,288,288]{2,1,0:T(8,128)(2,1)}, u32[]{:S(2)}) copy-start(bf16[1,288,288]{2,1,0:T(8,128)(2,1)} %copy.135) | copy-start | bytes 497668
  104.0 4.9 %copy-start.4 = (bf16[1,288,288]{2,1,0:T(8,128)(2,1)S(1)}, bf16[1,288,288]{2,1,0:T(8,128)(2,1)}, u32[]{:S(2)}) copy-start(bf16[1,288,288]{2,1,0:T(8,128)(2,1)} %copy.136) | copy-start | bytes 497668
  104.0 4.9 %copy-start.5 = (bf16[1,288,288]{2,1,0:T(8,128)(2,1)S(1)}, bf16[1,288,288]{2,1,0:T(8,128)(2,1)}, u32[]{:S(2)}) copy-start(bf16[1,288,288]{2,1,0:T(8,128)(2,1)} %copy.137) | copy-start | bytes 497668
  104.0 4.9 %copy-start.23 = (s32[288]{0:T(512)S(1)}, s32[288]{0:T(512)}, u32[]{:S(2)}) copy-start(s32[288]{0:T(512)} %fusion.34) | copy-start | bytes 3460
  104.0 6.3 %copy-start.8 = (bf16[3,2304]{1,0:T(4,128)(2,1)S(1)}, bf16[3,2304]{1,0:T(4,128)(2,1)}, u32[]{:S(2)}) copy-start(bf16[3,2304]{1,0:T(4,128)(2,1)} %convert_element_type.108) | copy-start | bytes 41476
  117.1 144.8 %copy-start.26 = (f32[3]{0:T(128)S(1)}, f32[3]{0:T(128)}, u32[]{:S(2)}) copy-start(f32[3]{0:T(128)} %convert_multiply_fusion.4) | copy-start | bytes 40
  117.1 144.9 %copy-start.10 = (f32[8,3]{0,1:T(4,128)S(1)}, f32[8,3]{0,1:T(4,128)}, u32[]{:S(2)}) copy-start(f32[8,3]{0,1:T(4,128)} %fusion.45) | copy-start | bytes 292
  262.1 3.7 %collective-permute-start = (f32[8,288]{1,0:T(8,128)S(1)}, f32[8,288]{1,0:T(8,128)S(1)}, u32[]{:S(2)}, u32[]{:S(2)}) collective-permute-start(f32[8,288]{1,0:T(8,128)S(1)} %multiply_reduce_fusion), channel_id=1, source_target_pairs={{0,1},{1,0},{2,3},{3,2},{4,5},{5,4},{6,7},{7,6},{8,9},{9,8},{10,11... | collective-permute-start | bytes 27656 | tf_op jit(solution)/shard_map/ppermute | solution.py:35
  265.8 4.6 %collective-permute-start.1 = (f32[4,288]{1,0:T(4,128)S(1)}, f32[4,288]{1,0:T(4,128)S(1)}, u32[]{:S(2)}, u32[]{:S(2)}) collective-permute-start(f32[4,288]{1,0:T(4,128)S(1)} %slice_select_fusion), channel_id=1, source_target_pairs={{0,8},{2,10},{4,12},{6,14},{8,0},{10,2},{12,4},{14,6},{1,9},{3,11}... | collective-permute-start | bytes 13832 | tf_op jit(solution)/shard_map/ppermute | solution.py:43
  270.4 3.7 %collective-permute-start.2 = (f32[2,288]{1,0:T(2,128)S(1)}, f32[2,288]{1,0:T(2,128)S(1)}, u32[]{:S(2)}, u32[]{:S(2)}) collective-permute-start(f32[2,288]{1,0:T(2,128)S(1)} %broadcast_select_fusion), channel_id=1, source_target_pairs={{0,4},{2,6},{4,0},{6,2},{8,12},{10,14},{12,8},{14,10},{1,5},{3,7},... | collective-permute-start | bytes 6920 | tf_op jit(solution)/shard_map/ppermute | solution.py:43
  274.1 1.2 collective-permute-start.3
  (9 other events, 29.8 us)
Sparse Core Ops, SparseCore 0:
  10.3 73.9 all-gather.1
